TPU v7x, 256 devices: a whole 4x4x8 slice. The times are simulated.
256 devices in a mesh: ctx: 32 (over y, x, core), tp: 8 (over z).
Axes of the slice: x: 4, y: 4, z: 8, core: 2. Of those that a mesh axis runs over, the one named last changes fastest.
Arguments:
- query: bfloat16 [8192, 4096], P('ctx', 'tp'), may hold values from -6 to 6
- keys: bfloat16 [8192, 4096], P('ctx', 'tp'), may hold values from -6 to 6
- values: bfloat16 [8192, 4096], P('ctx', 'tp'), may hold values from -6 to 6
- filt: float32 [8192, 4096], P('ctx', 'tp'), may hold values from -1 to 1
- direct: float32 [4096], P('tp'), may hold values from -4 to 4
- w_out: bfloat16 [4096, 4096], P('tp'), may hold values from -0.09375 to 0.09375
Outputs:
- output: bfloat16 [8192, 4096], P('ctx', 'tp')
All inputs are finite; a program needn't handle non-finite values.
Results may differ from a plain program's by a relative error of at most 0.0049.
Values sent between devices are 32-bit elements; how exact they have to be, the bound alone decides.
A program may use at most 128 MiB of HBM per device.

v0:
```python
import functools
import math

import jax
import jax.numpy as jnp
import numpy as np
from jax import lax
from jax.experimental import pallas as pl
from jax.experimental.pallas import tpu as pltpu
from jax.sharding import PartitionSpec as P

MESH = pl.DeviceIdType.MESH
F32 = jnp.float32
BF16 = jnp.bfloat16
LANES = 128
SUB = 8
CHUNKS = 2


def tables(block):
    order = np.concatenate([np.arange(0, block, 2), np.arange(1, block, 2)])
    place = np.arange(block)
    angle = math.pi * (2 * order[None, :] + 1) * place[:, None] / (2 * block)
    forward = np.concatenate([np.cos(angle), -np.sin(angle)], axis=1)
    inverse = np.concatenate([np.cos(angle.T), -np.sin(angle.T)], axis=0) / block
    out = []
    for table in (forward, inverse):
        high = table.astype(jnp.bfloat16)
        low = (table - high.astype(np.float64)).astype(jnp.bfloat16)
        out += [high, low]
    return out


def split(x):
    high = x.astype(BF16)
    return high, (x - high.astype(F32)).astype(BF16)


def dot3(x, high, low):
    xh, xl = split(x)
    total = jnp.dot(xh, low, preferred_element_type=F32)
    total += jnp.dot(xl, high, preferred_element_type=F32)
    return total + jnp.dot(xh, high, preferred_element_type=F32)


def kernel(
    nc, nz,
    q_hbm, k_hbm, v_hbm, f_hbm, d_hbm, w_hbm, th_hbm, tl_hbm, ih_hbm, il_hbm,
    o_ref,
    q, k, v, f, dr, w, th, tl, ih, il,
    sbuf, rbuf, sb, gb, zb, yb, cb, gated, snd, rcv,
    lsem, asend, arecv, bsend, brecv, zsend, zrecv,
):
    c = lax.axis_index("ctx")
    z = lax.axis_index("tp")
    block, chans = k.shape
    groups = sbuf.shape[0]
    width = groups * SUB

    loads = [
        pltpu.make_async_copy(src, dst, lsem.at[n])
        for n, (src, dst) in enumerate(
            [(k_hbm, k), (v_hbm, v), (f_hbm, f), (q_hbm, q), (d_hbm, dr), (th_hbm, th),
             (tl_hbm, tl), (ih_hbm, ih), (il_hbm, il), (w_hbm, w)]
        )
    ]
    for load in loads:
        load.start()

    barrier = pltpu.get_barrier_semaphore()

    def greet(d, _):
        pl.semaphore_signal(
            barrier, inc=1, device_id=(lax.rem(c + d, nc), z), device_id_type=MESH
        )
        return 0

    lax.fori_loop(1, nc, greet, 0)
    right, left = lax.rem(z + 1, nz), lax.rem(z + nz - 1, nz)
    for other in (right, left):
        pl.semaphore_signal(barrier, inc=1, device_id=(c, other), device_id_type=MESH)

    loads[0].wait()
    loads[1].wait()
    loads[2].wait()
    per = LANES // width
    for j in range(chans // LANES):
        cols = slice(j * LANES, (j + 1) * LANES)
        for which in range(2):
            if which == 0:
                part = k[:, cols].astype(F32) * v[:, cols].astype(F32)
            else:
                part = f[:, cols]
            part = part.T.reshape(per, groups, SUB, block)
            for g in range(groups):
                sbuf[g, which, j * per:(j + 1) * per] = part[:, g]
    for g in range(groups):
        rbuf[g, :, c] = sbuf[g, :, c]

    pl.semaphore_wait(barrier, nc + 1)

    def to_owner(g, d):
        t = lax.rem(c + d, nc)
        return pltpu.make_async_remote_copy(
            sbuf.at[g, :, t], rbuf.at[g, :, c], asend.at[g, d], arecv.at[g, d],
            device_id=(t, z), device_id_type=MESH,
        )

    def to_place(g, d):
        t = lax.rem(c + d, nc)
        rows = pl.ds(pl.multiple_of(c * width + g * SUB, SUB), SUB)
        return pltpu.make_async_remote_copy(
            yb.at[g, t], cb.at[rows], bsend.at[g, d], brecv.at[g, d],
            device_id=(t, z), device_id_type=MESH,
        )

    def each(make, act, g):
        def step(d, _):
            getattr(make(g, d), act)()
            return 0

        lax.fori_loop(1, nc, step, 0)

    for g in range(groups):
        each(to_owner, "start", g)
    for load in loads[3:]:
        load.wait()

    half = block // 2
    gb[:, :, 0:SUB] = jnp.zeros((2, 2, SUB, SUB, LANES), F32)
    for g in range(groups):
        each(to_owner, "wait_recv", g)
        flat = (nc * SUB, block)
        spec = dot3(rbuf[g, 0].reshape(flat), th[...], tl[...])
        for part in range(2):
            for tile in range(2):
                at = part * block + tile * half
                sb[tile, part] = spec[:, at:at + half].reshape(nc, SUB, LANES)
        spec = dot3(rbuf[g, 1].reshape(flat), th[...], tl[...])
        zero = jnp.zeros((1, SUB, LANES), F32)
        for tile in range(2):
            at = tile * half
            real = spec[:, at:at + half].reshape(nc, SUB, LANES)
            imag = spec[:, block + at:block + at + half].reshape(nc, SUB, LANES)
            real_b = jnp.concatenate([zero, real[:-1]], axis=0)
            imag_b = jnp.concatenate([zero, imag[:-1]], axis=0)
            if tile == 0:
                real, imag = real - imag_b, imag + real_b
            else:
                real, imag = real + imag_b, imag - real_b
            gb[tile, 0, SUB:] = real
            gb[tile, 1, SUB:] = imag

        def combine(tile, _):
            for hi in range(nc // SUB):
                acc_r = [None] * SUB
                acc_i = [None] * SUB
                for lo in range(hi + 1):
                    srcs = [(sb[tile, 0, lo * SUB + n], sb[tile, 1, lo * SUB + n]) for n in range(SUB)]
                    base = (hi - lo) * SUB
                    for diff in range(1 - SUB, SUB):
                        if base + diff < 0:
                            continue
                        fr = gb[tile, 0, SUB + base + diff]
                        fi = gb[tile, 1, SUB + base + diff]
                        for n in range(SUB):
                            a = n + diff
                            if a < 0 or a >= SUB:
                                continue
                            sr, si = srcs[n]
                            pr = sr * fr - si * fi
                            pi = sr * fi + si * fr
                            acc_r[a] = pr if acc_r[a] is None else acc_r[a] + pr
                            acc_i[a] = pi if acc_i[a] is None else acc_i[a] + pi
                for a in range(SUB):
                    zb[0, tile, hi * SUB + a] = acc_r[a]
                    zb[1, tile, hi * SUB + a] = acc_i[a]
            return 0

        lax.fori_loop(0, 2, combine, 0)
        whole = jnp.concatenate(
            [zb[p, t].reshape(nc * SUB, LANES) for p in range(2) for t in range(2)], axis=1
        )
        yb[g] = dot3(whole, ih[...], il[...]).reshape(nc, SUB, block)
        rows = pl.ds(pl.multiple_of(c * width + g * SUB, SUB), SUB)
        cb[rows] = yb[g, c]
        each(to_place, "start", g)
    for g in range(groups):
        each(to_place, "wait_recv", g)

    for j in range(chans // LANES):
        cols = slice(j * LANES, (j + 1) * LANES)
        signal = k[:, cols].astype(F32) * v[:, cols].astype(F32)
        conv = cb[cols, :].T
        gate = q[:, cols].astype(F32) * (conv + dr[:, cols] * signal)
        gated[:, cols] = gate.astype(BF16)

    out_cols = o_ref.shape[1]
    span = block // 2
    rows_of = span // CHUNKS

    def dest(way, s):
        step = nz - 1 - s if way == 0 else 1 + s
        return lax.rem(z + step, nz)

    def local(way, s):
        cols = pl.ds(pl.multiple_of(dest(way, s) * out_cols, out_cols), out_cols)
        return jnp.dot(
            gated[way * span:(way + 1) * span, :], w[:, cols], preferred_element_type=F32
        )

    def hop(way, part, s):
        return pltpu.make_async_remote_copy(
            snd.at[way, s, part], rcv.at[way, s, part],
            zsend.at[way, s, part], zrecv.at[way, s, part],
            device_id=(c, right if way == 0 else left), device_id_type=MESH,
        )

    for way in range(2):
        snd[way, 0] = local(way, 0).reshape(CHUNKS, rows_of, out_cols)
        for part in range(CHUNKS):
            hop(way, part, 0).start()

    def fill(s, _):
        for way in range(2):
            snd[way, s] = local(way, s).reshape(CHUNKS, rows_of, out_cols)
        return 0

    lax.fori_loop(1, nz, fill, 0)

    def ring(s, _):
        for part in range(CHUNKS):
            for way in range(2):
                hop(way, part, s - 1).wait_recv()
                snd[way, s, part] = snd[way, s, part] + rcv[way, s - 1, part]
                hop(way, part, s).start()
        return 0

    lax.fori_loop(1, nz - 1, ring, 0)
    for part in range(CHUNKS):
        for way in range(2):
            hop(way, part, nz - 2).wait_recv()
            at = way * span + part * rows_of
            o_ref[at:at + rows_of] = (snd[way, nz - 1, part] + rcv[way, nz - 2, part]).astype(BF16)

    for g in range(groups):
        each(to_owner, "wait_send", g)
        each(to_place, "wait_send", g)

    def drain(s, _):
        for way in range(2):
            for part in range(CHUNKS):
                hop(way, part, s).wait_send()
        return 0

    lax.fori_loop(0, nz - 1, drain, 0)


def solution(mesh):
    nc, nz = mesh.shape["ctx"], mesh.shape["tp"]

    def body(query, keys, values, filt, direct, w_out):
        block, chans = keys.shape
        out_cols = w_out.shape[1] // nz
        width = chans // nc
        groups = width // SUB
        rows_of = block // 2 // CHUNKS
        consts = [jnp.asarray(t) for t in tables(block)]
        operands = [query, keys, values, filt, direct.reshape(1, chans), w_out] + consts
        dma = pltpu.SemaphoreType.DMA
        return pl.pallas_call(
            functools.partial(kernel, nc, nz),
            out_shape=jax.ShapeDtypeStruct((block, out_cols), BF16),
            in_specs=[pl.BlockSpec(memory_space=pl.ANY)] * len(operands),
            out_specs=pl.BlockSpec(memory_space=pltpu.VMEM),
            scratch_shapes=[pltpu.VMEM(x.shape, x.dtype) for x in operands]
            + [
                pltpu.VMEM((groups, 2, nc, SUB, block), F32),
                pltpu.VMEM((groups, 2, nc, SUB, block), F32),
                pltpu.VMEM((2, 2, nc, SUB, LANES), F32),
                pltpu.VMEM((2, 2, nc + SUB, SUB, LANES), F32),
                pltpu.VMEM((2, 2, nc, SUB, LANES), F32),
                pltpu.VMEM((groups, nc, SUB, block), F32),
                pltpu.VMEM((chans, block), F32),
                pltpu.VMEM((block, chans), BF16),
                pltpu.VMEM((2, nz, CHUNKS, rows_of, out_cols), F32),
                pltpu.VMEM((2, nz - 1, CHUNKS, rows_of, out_cols), F32),
                dma((len(operands),)),
                dma((groups, nc)),
                dma((groups, nc)),
                dma((groups, nc)),
                dma((groups, nc)),
                dma((2, nz - 1, CHUNKS)),
                dma((2, nz - 1, CHUNKS)),
            ],
            compiler_params=pltpu.CompilerParams(
                collective_id=0, has_side_effects=True, vmem_limit_bytes=48 * 2**20
            ),
        )(*operands)

    return jax.shard_map(
        body,
        mesh=mesh,
        in_specs=(
            P("ctx", "tp"),
            P("ctx", "tp"),
            P("ctx", "tp"),
            P("ctx", "tp"),
            P("tp"),
            P("tp", None),
        ),
        out_specs=P("ctx", "tp"),
        check_vma=False,
    )
```

profile of v0, /device:TPU:1, one launch (start us, length us, event | category | flops | bytes accessed | tf_op | source)
XLA Modules:
  0.0 88.4 jit_solution(4968703717430744382)
XLA Ops:
  0.0 0.0 copy-start
  0.0 1.0 %copy-done = f32[256,512]{1,0:T(8,128)S(1)} copy-done((f32[256,512]{1,0:T(8,128)S(1)}, f32[256,512]{1,0:T(8,128)}, u32[]{:S(2)}) %copy-start) | copy-done | bytes 524312
  1.0 0.0 copy-start.1
  1.0 0.9 %copy-done.1 = bf16[256,512]{1,0:T(8,128)(2,1)S(1)} copy-done((bf16[256,512]{1,0:T(8,128)(2,1)S(1)}, bf16[256,512]{1,0:T(8,128)(2,1)}, u32[]{:S(2)}) %copy-start.1) | copy-done | bytes 262168
  2.0 0.0 copy-start.2
  2.0 0.9 %copy-done.2 = bf16[256,512]{1,0:T(8,128)(2,1)S(1)} copy-done((bf16[256,512]{1,0:T(8,128)(2,1)S(1)}, bf16[256,512]{1,0:T(8,128)(2,1)}, u32[]{:S(2)}) %copy-start.2) | copy-done | bytes 262168
  2.9 0.0 copy-start.3
  2.9 0.9 %copy-done.3 = bf16[256,512]{1,0:T(8,128)(2,1)S(1)} copy-done((bf16[256,512]{1,0:T(8,128)(2,1)S(1)}, bf16[256,512]{1,0:T(8,128)(2,1)}, u32[]{:S(2)}) %copy-start.3) | copy-done | bytes 262168
  3.9 0.0 copy-start.4
  3.9 0.9 %copy-done.4 = bf16[512,256]{1,0:T(8,128)(2,1)S(1)} copy-done((bf16[512,256]{1,0:T(8,128)(2,1)S(1)}, bf16[512,256]{1,0:T(8,128)(2,1)}, u32[]{:S(2)}) %copy-start.4) | copy-done | bytes 262168
  4.8 0.0 copy-start.5
  4.8 0.9 %copy-done.5 = bf16[512,256]{1,0:T(8,128)(2,1)S(1)} copy-done((bf16[512,256]{1,0:T(8,128)(2,1)S(1)}, bf16[512,256]{1,0:T(8,128)(2,1)}, u32[]{:S(2)}) %copy-start.5) | copy-done | bytes 262168
  5.8 0.0 copy-start.6
  5.8 0.9 %copy-done.6 = bf16[256,512]{1,0:T(8,128)(2,1)S(1)} copy-done((bf16[256,512]{1,0:T(8,128)(2,1)S(1)}, bf16[256,512]{1,0:T(8,128)(2,1)}, u32[]{:S(2)}) %copy-start.6) | copy-done | bytes 262168
  6.7 0.0 copy-start.7
  6.7 0.9 %copy-done.7 = bf16[256,512]{1,0:T(8,128)(2,1)S(1)} copy-done((bf16[256,512]{1,0:T(8,128)(2,1)S(1)}, bf16[256,512]{1,0:T(8,128)(2,1)}, u32[]{:S(2)}) %copy-start.7) | copy-done | bytes 262168
  7.7 0.0 copy-start.8
  7.7 0.7 copy-done.8
  8.4 79.3 %shard_map.100 = bf16[256,512]{1,0:T(8,128)(2,1)S(1)} custom-call(bf16[256,512]{1,0:T(8,128)(2,1)S(1)} %copy-done.1, bf16[256,512]{1,0:T(8,128)(2,1)S(1)} %copy-done.2, bf16[256,512]{1,0:T(8,128)(2,1)S(1)} %copy-done.3, f32[256,512]{1,0:T(8,128)S(1)} %copy-done, f32[1,512]{1,0:T(1,128)S(1)} %bitcast.1, bf16[512,4096]{1,0:T(8,128)(2,1)} %w_hbm.1, ...), custom_call_target="tpu_custom_call" | custom-call | tf_op jit(solution)/shard_map/pallas_call | solution.py:271
  87.7 0.7 copy.12
Async XLA Ops:
  0.0 1.0 %copy-start = (f32[256,512]{1,0:T(8,128)S(1)}, f32[256,512]{1,0:T(8,128)}, u32[]{:S(2)}) copy-start(f32[256,512]{1,0:T(8,128)} %f_hbm.1) | copy-start | bytes 1572868
  1.0 0.9 %copy-start.1 = (bf16[256,512]{1,0:T(8,128)(2,1)S(1)}, bf16[256,512]{1,0:T(8,128)(2,1)}, u32[]{:S(2)}) copy-start(bf16[256,512]{1,0:T(8,128)(2,1)} %q_hbm.1) | copy-start | bytes 786436
  2.0 0.9 %copy-start.2 = (bf16[256,512]{1,0:T(8,128)(2,1)S(1)}, bf16[256,512]{1,0:T(8,128)(2,1)}, u32[]{:S(2)}) copy-start(bf16[256,512]{1,0:T(8,128)(2,1)} %k_hbm.1) | copy-start | bytes 786436
  2.9 0.9 %copy-start.3 = (bf16[256,512]{1,0:T(8,128)(2,1)S(1)}, bf16[256,512]{1,0:T(8,128)(2,1)}, u32[]{:S(2)}) copy-start(bf16[256,512]{1,0:T(8,128)(2,1)} %v_hbm.1) | copy-start | bytes 786436
  3.9 0.9 %copy-start.4 = (bf16[512,256]{1,0:T(8,128)(2,1)S(1)}, bf16[512,256]{1,0:T(8,128)(2,1)}, u32[]{:S(2)}) copy-start(bf16[512,256]{1,0:T(8,128)(2,1)} %constant.11.clone.il_hbm) | copy-start | bytes 786436
  4.8 0.9 %copy-start.5 = (bf16[512,256]{1,0:T(8,128)(2,1)S(1)}, bf16[512,256]{1,0:T(8,128)(2,1)}, u32[]{:S(2)}) copy-start(bf16[512,256]{1,0:T(8,128)(2,1)} %constant.10.clone.ih_hbm) | copy-start | bytes 786436
  5.8 0.9 %copy-start.6 = (bf16[256,512]{1,0:T(8,128)(2,1)S(1)}, bf16[256,512]{1,0:T(8,128)(2,1)}, u32[]{:S(2)}) copy-start(bf16[256,512]{1,0:T(8,128)(2,1)} %constant.9.clone.tl_hbm) | copy-start | bytes 786436
  6.7 0.9 %copy-start.7 = (bf16[256,512]{1,0:T(8,128)(2,1)S(1)}, bf16[256,512]{1,0:T(8,128)(2,1)}, u32[]{:S(2)}) copy-start(bf16[256,512]{1,0:T(8,128)(2,1)} %constant.8.clone.th_hbm) | copy-start | bytes 786436
  7.7 0.7 copy-start.8
where the time goes:
time: 88.8 us; the launch traced here: 88.4 us
  Pallas kernels  79.3 us (89%)
  local copies, waits for them, and re-layouts  9.07 us (10%)
    pallas_call x1, Pallas kernels, body(): pl.pallas_call(functools.partial(kernel, nc, nz), out_shape=jax.ShapeDtyp...  79.3 us
    unnamed x19, local copies, waits for them, and re-layouts  9.07 us

commit v1 on v0

--- a/solution.py
+++ b/solution.py
@@ -14,7 +14,13 @@
 BF16 = jnp.bfloat16
 LANES = 128
 SUB = 8
-CHUNKS = 2
+PARTS = 2
+SIDE = 4
+NEAR = (0, 1, 2, -1)
+STEPS = sorted(
+    ((dx, dy, dk) for dx in NEAR for dy in NEAR for dk in (0, 1)),
+    key=lambda n: (abs(n[0]) + abs(n[1]), n[2]),
+)[:0:-1]
 
 
 def tables(block):
@@ -45,9 +51,9 @@
 
 def kernel(
     nc, nz,
-    q_hbm, k_hbm, v_hbm, f_hbm, d_hbm, w_hbm, th_hbm, tl_hbm, ih_hbm, il_hbm,
+    q_hbm, k_hbm, v_hbm, f_hbm, d_hbm, th_hbm, tl_hbm, ih_hbm, il_hbm, w_hbm,
     o_ref,
-    q, k, v, f, dr, w, th, tl, ih, il,
+    q, k, v, f, dr, th, tl, ih, il, w,
     sbuf, rbuf, sb, gb, zb, yb, cb, gated, snd, rcv,
     lsem, asend, arecv, bsend, brecv, zsend, zrecv,
 ):
@@ -55,13 +61,16 @@
     z = lax.axis_index("tp")
     block, chans = k.shape
     groups = sbuf.shape[0]
-    width = groups * SUB
+    gwide = chans // groups
+    out_cols = o_ref.shape[1]
+    half = block // 2
+    rows_of = half // PARTS
 
     loads = [
         pltpu.make_async_copy(src, dst, lsem.at[n])
         for n, (src, dst) in enumerate(
-            [(k_hbm, k), (v_hbm, v), (f_hbm, f), (q_hbm, q), (d_hbm, dr), (th_hbm, th),
-             (tl_hbm, tl), (ih_hbm, ih), (il_hbm, il), (w_hbm, w)]
+            [(k_hbm, k), (v_hbm, v), (f_hbm, f), (q_hbm, q), (d_hbm, dr),
+             (th_hbm, th), (tl_hbm, tl), (ih_hbm, ih), (il_hbm, il), (w_hbm, w)]
         )
     ]
     for load in loads:
@@ -83,52 +92,66 @@
     loads[0].wait()
     loads[1].wait()
     loads[2].wait()
-    per = LANES // width
+    per = LANES // SUB
     for j in range(chans // LANES):
         cols = slice(j * LANES, (j + 1) * LANES)
+        g, at = divmod(j * LANES, gwide)
+        at = at // SUB
         for which in range(2):
             if which == 0:
                 part = k[:, cols].astype(F32) * v[:, cols].astype(F32)
             else:
                 part = f[:, cols]
-            part = part.T.reshape(per, groups, SUB, block)
-            for g in range(groups):
-                sbuf[g, which, j * per:(j + 1) * per] = part[:, g]
+            sbuf[g, which, at:at + per] = part.T.reshape(per, SUB, block)
     for g in range(groups):
         rbuf[g, :, c] = sbuf[g, :, c]
-
     pl.semaphore_wait(barrier, nc + 1)
 
-    def to_owner(g, d):
-        t = lax.rem(c + d, nc)
+    core, px, py = lax.rem(c, 2), lax.rem(c // 2, SIDE), c // (2 * SIDE)
+
+    def partner(n):
+        dx, dy, dk = STEPS[n]
+        x, y = lax.rem(px + dx + SIDE, SIDE), lax.rem(py + dy + SIDE, SIDE)
+        return (y * SIDE + x) * 2 + lax.rem(core + dk, 2)
+
+    def to_owner(g, d, t):
         return pltpu.make_async_remote_copy(
             sbuf.at[g, :, t], rbuf.at[g, :, c], asend.at[g, d], arecv.at[g, d],
             device_id=(t, z), device_id_type=MESH,
         )
 
-    def to_place(g, d):
-        t = lax.rem(c + d, nc)
-        rows = pl.ds(pl.multiple_of(c * width + g * SUB, SUB), SUB)
+    def to_place(g, d, t):
         return pltpu.make_async_remote_copy(
-            yb.at[g, t], cb.at[rows], bsend.at[g, d], brecv.at[g, d],
+            yb.at[g, t], cb.at[g, c], bsend.at[g, d], brecv.at[g, d],
             device_id=(t, z), device_id_type=MESH,
         )
 
     def each(make, act, g):
         def step(d, _):
-            getattr(make(g, d), act)()
+            getattr(make(g, d, lax.rem(c + d + 1, nc)), act)()
             return 0
 
-        lax.fori_loop(1, nc, step, 0)
-
-    for g in range(groups):
-        each(to_owner, "start", g)
-    for load in loads[3:]:
+        lax.fori_loop(0, nc - 1, step, 0)
+
+    def hop(way, part, s):
+        return pltpu.make_async_remote_copy(
+            snd.at[way, s, part], rcv.at[way, s, part],
+            zsend.at[way, s, part], zrecv.at[way, s, part],
+            device_id=(c, right if way == 0 else left), device_id_type=MESH,
+        )
+
+    others = [partner(n) for n in range(nc - 1)]
+    for d, t in enumerate(others):
+        to_owner(0, d, t).start()
+    for load in loads[3:-1]:
         load.wait()
-
-    half = block // 2
+    for d, t in enumerate(others):
+        to_owner(0, d, t).wait_send()
+        to_owner(1, d, t).start()
+
     gb[:, :, 0:SUB] = jnp.zeros((2, 2, SUB, SUB, LANES), F32)
-    for g in range(groups):
+
+    def convolve(g):
         each(to_owner, "wait_recv", g)
         flat = (nc * SUB, block)
         spec = dot3(rbuf[g, 0].reshape(flat), th[...], tl[...])
@@ -182,54 +205,50 @@
             [zb[p, t].reshape(nc * SUB, LANES) for p in range(2) for t in range(2)], axis=1
         )
         yb[g] = dot3(whole, ih[...], il[...]).reshape(nc, SUB, block)
-        rows = pl.ds(pl.multiple_of(c * width + g * SUB, SUB), SUB)
-        cb[rows] = yb[g, c]
-        each(to_place, "start", g)
-    for g in range(groups):
+        cb[g, c] = yb[g, c]
+        for d, t in enumerate(others):
+            to_place(g, d, t).start()
+
+    def receive(g):
         each(to_place, "wait_recv", g)
-
-    for j in range(chans // LANES):
-        cols = slice(j * LANES, (j + 1) * LANES)
-        signal = k[:, cols].astype(F32) * v[:, cols].astype(F32)
-        conv = cb[cols, :].T
-        gate = q[:, cols].astype(F32) * (conv + dr[:, cols] * signal)
-        gated[:, cols] = gate.astype(BF16)
-
-    out_cols = o_ref.shape[1]
-    span = block // 2
-    rows_of = span // CHUNKS
-
-    def dest(way, s):
-        step = nz - 1 - s if way == 0 else 1 + s
-        return lax.rem(z + step, nz)
-
-    def local(way, s):
-        cols = pl.ds(pl.multiple_of(dest(way, s) * out_cols, out_cols), out_cols)
-        return jnp.dot(
-            gated[way * span:(way + 1) * span, :], w[:, cols], preferred_element_type=F32
-        )
-
-    def hop(way, part, s):
-        return pltpu.make_async_remote_copy(
-            snd.at[way, s, part], rcv.at[way, s, part],
-            zsend.at[way, s, part], zrecv.at[way, s, part],
-            device_id=(c, right if way == 0 else left), device_id_type=MESH,
-        )
-
-    for way in range(2):
-        snd[way, 0] = local(way, 0).reshape(CHUNKS, rows_of, out_cols)
-        for part in range(CHUNKS):
-            hop(way, part, 0).start()
+        for j in range(gwide // LANES):
+            rows = cb[g, j * per:(j + 1) * per].reshape(LANES, block)
+            cols = slice(g * gwide + j * LANES, g * gwide + (j + 1) * LANES)
+            signal = k[:, cols].astype(F32) * v[:, cols].astype(F32)
+            gate = q[:, cols].astype(F32) * (rows.T + dr[:, cols] * signal)
+            gated[:, cols] = gate.astype(BF16)
+
+    def local(g, way, s):
+        dest = lax.rem(z + (nz - 1 - s if way == 0 else 1 + s), nz)
+        cols = pl.ds(pl.multiple_of(dest * out_cols, out_cols), out_cols)
+        terms = jnp.dot(
+            gated[way * half:(way + 1) * half, g * gwide:(g + 1) * gwide],
+            w[g * gwide:(g + 1) * gwide, cols],
+            preferred_element_type=F32,
+        ).reshape(PARTS, rows_of, out_cols)
+        snd[way, s] = terms if g == 0 else snd[way, s] + terms
+
+    convolve(0)
+    convolve(1)
+    loads[-1].wait()
+    receive(0)
 
     def fill(s, _):
         for way in range(2):
-            snd[way, s] = local(way, s).reshape(CHUNKS, rows_of, out_cols)
+            local(0, way, s)
         return 0
 
-    lax.fori_loop(1, nz, fill, 0)
+    lax.fori_loop(0, nz, fill, 0)
+    receive(1)
+    for way in range(2):
+        local(1, way, 0)
+        for part in range(PARTS):
+            hop(way, part, 0).start()
 
     def ring(s, _):
-        for part in range(CHUNKS):
+        for way in range(2):
+            local(1, way, s)
+        for part in range(PARTS):
             for way in range(2):
                 hop(way, part, s - 1).wait_recv()
                 snd[way, s, part] = snd[way, s, part] + rcv[way, s - 1, part]
@@ -237,19 +256,21 @@
         return 0
 
     lax.fori_loop(1, nz - 1, ring, 0)
-    for part in range(CHUNKS):
+    for way in range(2):
+        local(1, way, nz - 1)
+    for part in range(PARTS):
         for way in range(2):
             hop(way, part, nz - 2).wait_recv()
-            at = way * span + part * rows_of
+            at = way * half + part * rows_of
             o_ref[at:at + rows_of] = (snd[way, nz - 1, part] + rcv[way, nz - 2, part]).astype(BF16)
 
+    each(to_owner, "wait_send", 1)
     for g in range(groups):
-        each(to_owner, "wait_send", g)
         each(to_place, "wait_send", g)
 
     def drain(s, _):
         for way in range(2):
-            for part in range(CHUNKS):
+            for part in range(PARTS):
                 hop(way, part, s).wait_send()
         return 0
 
@@ -262,18 +283,20 @@
     def body(query, keys, values, filt, direct, w_out):
         block, chans = keys.shape
         out_cols = w_out.shape[1] // nz
-        width = chans // nc
-        groups = width // SUB
-        rows_of = block // 2 // CHUNKS
+        groups = chans // nc // SUB
+        gwide = chans // groups
         consts = [jnp.asarray(t) for t in tables(block)]
-        operands = [query, keys, values, filt, direct.reshape(1, chans), w_out] + consts
+        operands = [query, keys, values, filt, direct.reshape(1, chans)] + consts + [w_out]
+        rows_of = block // 2 // PARTS
+        copies = [pltpu.VMEM(x.shape, x.dtype) for x in operands]
         dma = pltpu.SemaphoreType.DMA
+        operands = [pltpu.with_memory_space_constraint(x, pltpu.HBM) for x in operands]
         return pl.pallas_call(
             functools.partial(kernel, nc, nz),
             out_shape=jax.ShapeDtypeStruct((block, out_cols), BF16),
-            in_specs=[pl.BlockSpec(memory_space=pl.ANY)] * len(operands),
+            in_specs=[pl.BlockSpec(memory_space=pltpu.HBM)] * len(operands),
             out_specs=pl.BlockSpec(memory_space=pltpu.VMEM),
-            scratch_shapes=[pltpu.VMEM(x.shape, x.dtype) for x in operands]
+            scratch_shapes=copies
             + [
                 pltpu.VMEM((groups, 2, nc, SUB, block), F32),
                 pltpu.VMEM((groups, 2, nc, SUB, block), F32),
@@ -281,17 +304,17 @@
                 pltpu.VMEM((2, 2, nc + SUB, SUB, LANES), F32),
                 pltpu.VMEM((2, 2, nc, SUB, LANES), F32),
                 pltpu.VMEM((groups, nc, SUB, block), F32),
-                pltpu.VMEM((chans, block), F32),
+                pltpu.VMEM((groups, nc, SUB, block), F32),
                 pltpu.VMEM((block, chans), BF16),
-                pltpu.VMEM((2, nz, CHUNKS, rows_of, out_cols), F32),
-                pltpu.VMEM((2, nz - 1, CHUNKS, rows_of, out_cols), F32),
+                pltpu.VMEM((2, nz, PARTS, rows_of, out_cols), F32),
+                pltpu.VMEM((2, nz - 1, PARTS, rows_of, out_cols), F32),
                 dma((len(operands),)),
                 dma((groups, nc)),
                 dma((groups, nc)),
                 dma((groups, nc)),
                 dma((groups, nc)),
-                dma((2, nz - 1, CHUNKS)),
-                dma((2, nz - 1, CHUNKS)),
+                dma((2, nz - 1, PARTS)),
+                dma((2, nz - 1, PARTS)),
             ],
             compiler_params=pltpu.CompilerParams(
                 collective_id=0, has_side_effects=True, vmem_limit_bytes=48 * 2**20

time: 88.8 us -> 79.2 us (0.89)
  local copies, waits for them, and re-layouts: 9.07 us -> 0.71 us
  Pallas kernels: 79.3 us -> 78.4 us
    unnamed x19 -> x1, local copies, waits for them, and re-layouts: 9.07 us -> 0.71 us
    pallas_call x1, Pallas kernels: 79.3 us -> 78.4 us  [body(): pl.pallas_call(functools.partial(kernel, nc, nz), out_shape=jax.ShapeDtyp...]
where the time goes in v1:
time: 79.2 us; the launch traced here: 79.1 us
  Pallas kernels  78.4 us (99%)
    pallas_call x1, Pallas kernels, body(): pl.pallas_call(functools.partial(kernel, nc, nz), out_shape=jax.ShapeDtyp...  78.4 us

profile of v1, /device:TPU:1, one launch (start us, length us, event | category | flops | bytes accessed | tf_op | source)
XLA Modules:
  0.0 79.1 jit_solution(13982916254247761316)
XLA Ops:
  0.0 78.4 %shard_map.100 = bf16[256,512]{1,0:T(8,128)(2,1)S(1)} custom-call(bf16[256,512]{1,0:T(8,128)(2,1)} %q_hbm.1, bf16[256,512]{1,0:T(8,128)(2,1)} %k_hbm.1, bf16[256,512]{1,0:T(8,128)(2,1)} %v_hbm.1, f32[256,512]{1,0:T(8,128)} %f_hbm.1, f32[1,512]{1,0:T(1,128)} %bitcast.1, bf16[256,512]{1,0:T(8,128)(2,1)} %constant.8.clone.th_hbm, ...), custom_call_target="tpu_custom_call" | custom-call | tf_op jit(solution)/shard_map/pallas_call | solution.py:294
  78.4 0.7 copy.12

commit v2 on v1

--- a/solution.py
+++ b/solution.py
@@ -73,7 +73,7 @@
              (th_hbm, th), (tl_hbm, tl), (ih_hbm, ih), (il_hbm, il), (w_hbm, w)]
         )
     ]
-    for load in loads:
+    for load in loads[:3]:
         load.start()
 
     barrier = pltpu.get_barrier_semaphore()
@@ -114,45 +114,61 @@
         x, y = lax.rem(px + dx + SIDE, SIDE), lax.rem(py + dy + SIDE, SIDE)
         return (y * SIDE + x) * 2 + lax.rem(core + dk, 2)
 
-    def to_owner(g, d, t):
-        return pltpu.make_async_remote_copy(
-            sbuf.at[g, :, t], rbuf.at[g, :, c], asend.at[g, d], arecv.at[g, d],
+    def to_owner(g, t):
+        return pltpu.make_async_remote_copy(
+            sbuf.at[g, :, t], rbuf.at[g, :, c], asend.at[g], arecv.at[g],
             device_id=(t, z), device_id_type=MESH,
         )
 
-    def to_place(g, d, t):
-        return pltpu.make_async_remote_copy(
-            yb.at[g, t], cb.at[g, c], bsend.at[g, d], brecv.at[g, d],
+    def to_place(g, t):
+        return pltpu.make_async_remote_copy(
+            yb.at[g, t], cb.at[g, c], bsend.at[g], brecv.at[g],
             device_id=(t, z), device_id_type=MESH,
         )
 
-    def each(make, act, g):
-        def step(d, _):
-            getattr(make(g, d, lax.rem(c + d + 1, nc)), act)()
-            return 0
-
-        lax.fori_loop(0, nc - 1, step, 0)
+    def all_owner(g):
+        blocks = pl.ds(0, nc - 1)
+        return pltpu.make_async_remote_copy(
+            sbuf.at[g, :, blocks], rbuf.at[g, :, blocks], asend.at[g], arecv.at[g],
+            device_id=(others[0], z), device_id_type=MESH,
+        )
+
+    def all_place(g):
+        blocks = pl.ds(0, nc - 1)
+        return pltpu.make_async_remote_copy(
+            yb.at[g, blocks], cb.at[g, blocks], bsend.at[g], brecv.at[g],
+            device_id=(others[0], z), device_id_type=MESH,
+        )
+
+    def all_hops():
+        steps = pl.ds(0, nz - 1)
+        return pltpu.make_async_remote_copy(
+            snd.at[:, steps], rcv, zsend.at[0], zrecv.at[0, 0, 0],
+            device_id=(c, right), device_id_type=MESH,
+        )
 
     def hop(way, part, s):
         return pltpu.make_async_remote_copy(
             snd.at[way, s, part], rcv.at[way, s, part],
-            zsend.at[way, s, part], zrecv.at[way, s, part],
+            zsend.at[0], zrecv.at[way, s, part],
             device_id=(c, right if way == 0 else left), device_id_type=MESH,
         )
 
     others = [partner(n) for n in range(nc - 1)]
-    for d, t in enumerate(others):
-        to_owner(0, d, t).start()
+    for t in others:
+        to_owner(0, t).start()
+    for load in loads[3:]:
+        load.start()
     for load in loads[3:-1]:
         load.wait()
-    for d, t in enumerate(others):
-        to_owner(0, d, t).wait_send()
-        to_owner(1, d, t).start()
+    all_owner(0).wait_send()
+    for t in others:
+        to_owner(1, t).start()
 
     gb[:, :, 0:SUB] = jnp.zeros((2, 2, SUB, SUB, LANES), F32)
 
     def convolve(g):
-        each(to_owner, "wait_recv", g)
+        all_owner(g).wait_recv()
         flat = (nc * SUB, block)
         spec = dot3(rbuf[g, 0].reshape(flat), th[...], tl[...])
         for part in range(2):
@@ -206,11 +222,11 @@
         )
         yb[g] = dot3(whole, ih[...], il[...]).reshape(nc, SUB, block)
         cb[g, c] = yb[g, c]
-        for d, t in enumerate(others):
-            to_place(g, d, t).start()
+        for t in others:
+            to_place(g, t).start()
 
     def receive(g):
-        each(to_place, "wait_recv", g)
+        all_place(g).wait_recv()
         for j in range(gwide // LANES):
             rows = cb[g, j * per:(j + 1) * per].reshape(LANES, block)
             cols = slice(g * gwide + j * LANES, g * gwide + (j + 1) * LANES)
@@ -264,17 +280,10 @@
             at = way * half + part * rows_of
             o_ref[at:at + rows_of] = (snd[way, nz - 1, part] + rcv[way, nz - 2, part]).astype(BF16)
 
-    each(to_owner, "wait_send", 1)
+    all_owner(1).wait_send()
     for g in range(groups):
-        each(to_place, "wait_send", g)
-
-    def drain(s, _):
-        for way in range(2):
-            for part in range(PARTS):
-                hop(way, part, s).wait_send()
-        return 0
-
-    lax.fori_loop(0, nz - 1, drain, 0)
+        all_place(g).wait_send()
+    all_hops().wait_send()
 
 
 def solution(mesh):
@@ -309,11 +318,11 @@
                 pltpu.VMEM((2, nz, PARTS, rows_of, out_cols), F32),
                 pltpu.VMEM((2, nz - 1, PARTS, rows_of, out_cols), F32),
                 dma((len(operands),)),
-                dma((groups, nc)),
-                dma((groups, nc)),
-                dma((groups, nc)),
-                dma((groups, nc)),
-                dma((2, nz - 1, PARTS)),
+                dma((groups,)),
+                dma((groups,)),
+                dma((groups,)),
+                dma((groups,)),
+                dma((1,)),
                 dma((2, nz - 1, PARTS)),
             ],
             compiler_params=pltpu.CompilerParams(

time: 79.2 us -> 75.5 us (0.953)
  Pallas kernels: 78.4 us -> 74.7 us
    pallas_call x1, Pallas kernels: 78.4 us -> 74.7 us  [body(): pl.pallas_call(functools.partial(kernel, nc, nz), out_shape=jax.ShapeDtyp...]
where the time goes in v2:
time: 75.5 us; the launch traced here: 75.4 us
  Pallas kernels  74.7 us (99%)
    pallas_call x1, Pallas kernels, body(): pl.pallas_call(functools.partial(kernel, nc, nz), out_shape=jax.ShapeDtyp...  74.7 us

profile of v2, /device:TPU:1, one launch (start us, length us, event | category | flops | bytes accessed | tf_op | source)
XLA Modules:
  0.0 75.4 jit_solution(4014377340783685197)
XLA Ops:
  0.0 74.7 %shard_map.100 = bf16[256,512]{1,0:T(8,128)(2,1)S(1)} custom-call(bf16[256,512]{1,0:T(8,128)(2,1)} %q_hbm.1, bf16[256,512]{1,0:T(8,128)(2,1)} %k_hbm.1, bf16[256,512]{1,0:T(8,128)(2,1)} %v_hbm.1, f32[256,512]{1,0:T(8,128)} %f_hbm.1, f32[1,512]{1,0:T(1,128)} %bitcast.1, bf16[256,512]{1,0:T(8,128)(2,1)} %constant.8.clone.th_hbm, ...), custom_call_target="tpu_custom_call" | custom-call | tf_op jit(solution)/shard_map/pallas_call | solution.py:303
  74.7 0.7 copy.12

commit v3 on v2

--- a/solution.py
+++ b/solution.py
@@ -54,8 +54,8 @@
     q_hbm, k_hbm, v_hbm, f_hbm, d_hbm, th_hbm, tl_hbm, ih_hbm, il_hbm, w_hbm,
     o_ref,
     q, k, v, f, dr, th, tl, ih, il, w,
-    sbuf, rbuf, sb, gb, zb, yb, cb, gated, snd, rcv,
-    lsem, asend, arecv, bsend, brecv, zsend, zrecv,
+    sbuf, rbuf, sb, gb, zb, yb, cb, gated, snd, rcv, wown, wfar, wnext, gown, gfar,
+    lsem, asend, arecv, bsend, brecv, zsend, zrecv, wsend, wrecv, gsend, grecv,
 ):
     c = lax.axis_index("ctx")
     z = lax.axis_index("tp")
@@ -141,17 +141,49 @@
         )
 
     def all_hops():
-        steps = pl.ds(0, nz - 1)
-        return pltpu.make_async_remote_copy(
-            snd.at[:, steps], rcv, zsend.at[0], zrecv.at[0, 0, 0],
+        steps = pl.ds(1, nz - 2)
+        return pltpu.make_async_remote_copy(
+            snd.at[:, steps], rcv.at[:, steps], zsend.at[0], zrecv.at[0, 0, 0],
             device_id=(c, right), device_id_type=MESH,
         )
 
     def hop(way, part, s):
         return pltpu.make_async_remote_copy(
             snd.at[way, s, part], rcv.at[way, s, part],
-            zsend.at[0], zrecv.at[way, s, part],
+            zsend.at[0], zrecv.at[way, s - 1, part],
             device_id=(c, right if way == 0 else left), device_id_type=MESH,
+        )
+
+    sibling = c + 1 - 2 * core
+    wrows = pl.ds(pl.multiple_of(core * gwide, gwide), gwide)
+
+    def block_of(step):
+        at = lax.rem(z + nz + step, nz) * out_cols
+        return pl.ds(pl.multiple_of(at, out_cols), out_cols)
+
+    def to_next(way):
+        return pltpu.make_async_remote_copy(
+            wown.at[way], wfar.at[way, wrows], wsend.at[way], wrecv.at[way],
+            device_id=(c, right if way == 0 else left), device_id_type=MESH,
+        )
+
+    def to_sibling():
+        rows = wfar.at[:, wrows]
+        return pltpu.make_async_remote_copy(
+            rows, rows, wsend.at[2], wrecv.at[2], device_id=(sibling, z), device_id_type=MESH
+        )
+
+    def gated_hop(way, g, part):
+        return pltpu.make_async_remote_copy(
+            gown.at[way, g, part], gfar.at[way, g, part],
+            gsend.at[0], grecv.at[way, g, part],
+            device_id=(c, right if way == 0 else left), device_id_type=MESH,
+        )
+
+    def all_gated():
+        return pltpu.make_async_remote_copy(
+            gown, gfar, gsend.at[0], grecv.at[0, 0, 0],
+            device_id=(c, right), device_id_type=MESH,
         )
 
     others = [partner(n) for n in range(nc - 1)]
@@ -164,6 +196,10 @@
     all_owner(0).wait_send()
     for t in others:
         to_owner(1, t).start()
+    loads[-1].wait()
+    for way in range(2):
+        wown[way] = w[wrows, block_of(1 if way else -1)].astype(F32)
+        to_next(way).start()
 
     gb[:, :, 0:SUB] = jnp.zeros((2, 2, SUB, SUB, LANES), F32)
 
@@ -232,7 +268,13 @@
             cols = slice(g * gwide + j * LANES, g * gwide + (j + 1) * LANES)
             signal = k[:, cols].astype(F32) * v[:, cols].astype(F32)
             gate = q[:, cols].astype(F32) * (rows.T + dr[:, cols] * signal)
-            gated[:, cols] = gate.astype(BF16)
+            gate = gate.astype(BF16)
+            gated[:, cols] = gate
+            gate = gate.astype(F32).reshape(2, PARTS, rows_of, LANES)
+            gown[:, g, :, :, j * LANES:(j + 1) * LANES] = gate
+        for part in range(PARTS):
+            for way in range(2):
+                gated_hop(way, g, part).start()
 
     def local(g, way, s):
         dest = lax.rem(z + (nz - 1 - s if way == 0 else 1 + s), nz)
@@ -246,7 +288,9 @@
 
     convolve(0)
     convolve(1)
-    loads[-1].wait()
+    for way in range(2):
+        to_next(way).wait_recv()
+    to_sibling().start()
     receive(0)
 
     def fill(s, _):
@@ -254,12 +298,25 @@
             local(0, way, s)
         return 0
 
-    lax.fori_loop(0, nz, fill, 0)
+    lax.fori_loop(1, nz, fill, 0)
+    to_sibling().wait_recv()
+    wnext[...] = wfar[...].astype(BF16)
+    for way in range(2):
+        for part in range(PARTS):
+            gated_hop(way, 0, part).wait_recv()
+            snd[way, 1, part] = snd[way, 1, part] + jnp.dot(
+                gfar[way, 0, part].astype(BF16), wnext[way, :gwide], preferred_element_type=F32
+            )
     receive(1)
     for way in range(2):
-        local(1, way, 0)
-        for part in range(PARTS):
-            hop(way, part, 0).start()
+        local(1, way, 1)
+    for part in range(PARTS):
+        for way in range(2):
+            gated_hop(way, 1, part).wait_recv()
+            snd[way, 1, part] = snd[way, 1, part] + jnp.dot(
+                gfar[way, 1, part].astype(BF16), wnext[way, gwide:], preferred_element_type=F32
+            )
+            hop(way, part, 1).start()
 
     def ring(s, _):
         for way in range(2):
@@ -271,7 +328,7 @@
                 hop(way, part, s).start()
         return 0
 
-    lax.fori_loop(1, nz - 1, ring, 0)
+    lax.fori_loop(2, nz - 1, ring, 0)
     for way in range(2):
         local(1, way, nz - 1)
     for part in range(PARTS):
@@ -284,6 +341,10 @@
     for g in range(groups):
         all_place(g).wait_send()
     all_hops().wait_send()
+    all_gated().wait_send()
+    for way in range(2):
+        to_next(way).wait_send()
+    to_sibling().wait_send()
 
 
 def solution(mesh):
@@ -317,13 +378,22 @@
                 pltpu.VMEM((block, chans), BF16),
                 pltpu.VMEM((2, nz, PARTS, rows_of, out_cols), F32),
                 pltpu.VMEM((2, nz - 1, PARTS, rows_of, out_cols), F32),
+                pltpu.VMEM((2, gwide, out_cols), F32),
+                pltpu.VMEM((2, chans, out_cols), F32),
+                pltpu.VMEM((2, chans, out_cols), BF16),
+                pltpu.VMEM((2, groups, PARTS, rows_of, gwide), F32),
+                pltpu.VMEM((2, groups, PARTS, rows_of, gwide), F32),
                 dma((len(operands),)),
                 dma((groups,)),
                 dma((groups,)),
                 dma((groups,)),
                 dma((groups,)),
                 dma((1,)),
-                dma((2, nz - 1, PARTS)),
+                dma((2, nz - 2, PARTS)),
+                dma((3,)),
+                dma((3,)),
+                dma((1,)),
+                dma((2, groups, PARTS)),
             ],
             compiler_params=pltpu.CompilerParams(
                 collective_id=0, has_side_effects=True, vmem_limit_bytes=48 * 2**20

time: 75.5 us -> 73.9 us (0.979); the launches traced: 75.4 us -> 72.9 us
  Pallas kernels: 74.7 us -> 72.2 us
    pallas_call x1, Pallas kernels: 74.7 us -> 72.2 us  [body(): pl.pallas_call(functools.partial(kernel, nc, nz), out_shape=jax.ShapeDtyp...]
where the time goes in v3:
time: 73.9 us; the launch traced here: 72.9 us
  Pallas kernels  72.2 us (98%)
    pallas_call x1, Pallas kernels, body(): pl.pallas_call(functools.partial(kernel, nc, nz), out_shape=jax.ShapeDtyp...  72.2 us

profile of v3, /device:TPU:1, one launch (start us, length us, event | category | flops | bytes accessed | tf_op | source)
XLA Modules:
  0.0 72.9 jit_solution(18315993036052653914)
XLA Ops:
  0.0 72.2 %shard_map.100 = bf16[256,512]{1,0:T(8,128)(2,1)S(1)} custom-call(bf16[256,512]{1,0:T(8,128)(2,1)} %q_hbm.1, bf16[256,512]{1,0:T(8,128)(2,1)} %k_hbm.1, bf16[256,512]{1,0:T(8,128)(2,1)} %v_hbm.1, f32[256,512]{1,0:T(8,128)} %f_hbm.1, f32[1,512]{1,0:T(1,128)} %bitcast.1, bf16[256,512]{1,0:T(8,128)(2,1)} %constant.8.clone.th_hbm, ...), custom_call_target="tpu_custom_call" | custom-call | tf_op jit(solution)/shard_map/pallas_call | solution.py:364
  72.2 0.7 copy.12

commit v4 on v3

--- a/solution.py
+++ b/solution.py
@@ -14,7 +14,7 @@
 BF16 = jnp.bfloat16
 LANES = 128
 SUB = 8
-PARTS = 2
+PARTS = 4
 SIDE = 4
 NEAR = (0, 1, 2, -1)
 STEPS = sorted(
@@ -54,7 +54,7 @@
     q_hbm, k_hbm, v_hbm, f_hbm, d_hbm, th_hbm, tl_hbm, ih_hbm, il_hbm, w_hbm,
     o_ref,
     q, k, v, f, dr, th, tl, ih, il, w,
-    sbuf, rbuf, sb, gb, zb, yb, cb, gated, snd, rcv, wown, wfar, wnext, gown, gfar,
+    sbuf, rbuf, sb, gb, zb, yb, cb, gated, snd, rcv, wpart, wown, wfar, wnext, gown, gfar,
     lsem, asend, arecv, bsend, brecv, zsend, zrecv, wsend, wrecv, gsend, grecv,
 ):
     c = lax.axis_index("ctx")
@@ -66,6 +66,15 @@
     half = block // 2
     rows_of = half // PARTS
 
+    core, px, py = lax.rem(c, 2), lax.rem(c // 2, SIDE), c // (2 * SIDE)
+
+    sibling = c + 1 - 2 * core
+    wrows = pl.ds(pl.multiple_of(core * gwide, gwide), gwide)
+
+    def block_of(step):
+        at = lax.rem(z + nz + step, nz) * out_cols
+        return pl.ds(pl.multiple_of(at, out_cols), out_cols)
+
     loads = [
         pltpu.make_async_copy(src, dst, lsem.at[n])
         for n, (src, dst) in enumerate(
@@ -73,7 +82,13 @@
              (th_hbm, th), (tl_hbm, tl), (ih_hbm, ih), (il_hbm, il), (w_hbm, w)]
         )
     ]
-    for load in loads[:3]:
+    first = [
+        pltpu.make_async_copy(
+            w_hbm.at[wrows, block_of(1 if way else -1)], wpart.at[way], lsem.at[len(loads) + way]
+        )
+        for way in range(2)
+    ]
+    for load in loads[:3] + first:
         load.start()
 
     barrier = pltpu.get_barrier_semaphore()
@@ -105,9 +120,10 @@
             sbuf[g, which, at:at + per] = part.T.reshape(per, SUB, block)
     for g in range(groups):
         rbuf[g, :, c] = sbuf[g, :, c]
+    for way in range(2):
+        first[way].wait()
+        wown[way] = wpart[way].astype(F32)
     pl.semaphore_wait(barrier, nc + 1)
-
-    core, px, py = lax.rem(c, 2), lax.rem(c // 2, SIDE), c // (2 * SIDE)
 
     def partner(n):
         dx, dy, dk = STEPS[n]
@@ -154,13 +170,6 @@
             device_id=(c, right if way == 0 else left), device_id_type=MESH,
         )
 
-    sibling = c + 1 - 2 * core
-    wrows = pl.ds(pl.multiple_of(core * gwide, gwide), gwide)
-
-    def block_of(step):
-        at = lax.rem(z + nz + step, nz) * out_cols
-        return pl.ds(pl.multiple_of(at, out_cols), out_cols)
-
     def to_next(way):
         return pltpu.make_async_remote_copy(
             wown.at[way], wfar.at[way, wrows], wsend.at[way], wrecv.at[way],
@@ -189,6 +198,8 @@
     others = [partner(n) for n in range(nc - 1)]
     for t in others:
         to_owner(0, t).start()
+    for way in range(2):
+        to_next(way).start()
     for load in loads[3:]:
         load.start()
     for load in loads[3:-1]:
@@ -196,10 +207,6 @@
     all_owner(0).wait_send()
     for t in others:
         to_owner(1, t).start()
-    loads[-1].wait()
-    for way in range(2):
-        wown[way] = w[wrows, block_of(1 if way else -1)].astype(F32)
-        to_next(way).start()
 
     gb[:, :, 0:SUB] = jnp.zeros((2, 2, SUB, SUB, LANES), F32)
 
@@ -291,6 +298,7 @@
     for way in range(2):
         to_next(way).wait_recv()
     to_sibling().start()
+    loads[-1].wait()
     receive(0)
 
     def fill(s, _):
@@ -378,12 +386,13 @@
                 pltpu.VMEM((block, chans), BF16),
                 pltpu.VMEM((2, nz, PARTS, rows_of, out_cols), F32),
                 pltpu.VMEM((2, nz - 1, PARTS, rows_of, out_cols), F32),
+                pltpu.VMEM((2, gwide, out_cols), BF16),
                 pltpu.VMEM((2, gwide, out_cols), F32),
                 pltpu.VMEM((2, chans, out_cols), F32),
                 pltpu.VMEM((2, chans, out_cols), BF16),
                 pltpu.VMEM((2, groups, PARTS, rows_of, gwide), F32),
                 pltpu.VMEM((2, groups, PARTS, rows_of, gwide), F32),
-                dma((len(operands),)),
+                dma((len(operands) + 2,)),
                 dma((groups,)),
                 dma((groups,)),
                 dma((groups,)),

time: 73.9 us -> 73.4 us (level); the launches traced: 72.9 us -> 73.3 us
  no operation moved by 1% of the time
where the time goes in v4:
time: 73.4 us; the launch traced here: 73.3 us
  Pallas kernels  72.6 us (99%)
    pallas_call x1, Pallas kernels, body(): pl.pallas_call(functools.partial(kernel, nc, nz), out_shape=jax.ShapeDtyp...  72.6 us

profile of v4, /device:TPU:1, one launch (start us, length us, event | category | flops | bytes accessed | tf_op | source)
XLA Modules:
  0.0 73.3 jit_solution(17581207715144415126)
XLA Ops:
  0.0 72.6 %shard_map.100 = bf16[256,512]{1,0:T(8,128)(2,1)S(1)} custom-call(bf16[256,512]{1,0:T(8,128)(2,1)} %q_hbm.1, bf16[256,512]{1,0:T(8,128)(2,1)} %k_hbm.1, bf16[256,512]{1,0:T(8,128)(2,1)} %v_hbm.1, f32[256,512]{1,0:T(8,128)} %f_hbm.1, f32[1,512]{1,0:T(1,128)} %bitcast.1, bf16[256,512]{1,0:T(8,128)(2,1)} %constant.8.clone.th_hbm, ...), custom_call_target="tpu_custom_call" | custom-call | tf_op jit(solution)/shard_map/pallas_call | solution.py:372
  72.6 0.7 copy.12

commit v5 on v4

--- a/solution.py
+++ b/solution.py
@@ -68,6 +68,20 @@
 
     core, px, py = lax.rem(c, 2), lax.rem(c // 2, SIDE), c // (2 * SIDE)
 
+    barrier = pltpu.get_barrier_semaphore()
+
+    def partner(n):
+        dx, dy, dk = STEPS[n]
+        x, y = lax.rem(px + dx + SIDE, SIDE), lax.rem(py + dy + SIDE, SIDE)
+        return (y * SIDE + x) * 2 + lax.rem(core + dk, 2)
+
+    others = [partner(n) for n in range(nc - 1)]
+    for t in others:
+        pl.semaphore_signal(barrier, inc=1, device_id=(t, z), device_id_type=MESH)
+    right, left = lax.rem(z + 1, nz), lax.rem(z + nz - 1, nz)
+    for other in (right, left):
+        pl.semaphore_signal(barrier, inc=1, device_id=(c, other), device_id_type=MESH)
+
     sibling = c + 1 - 2 * core
     wrows = pl.ds(pl.multiple_of(core * gwide, gwide), gwide)
 
@@ -90,19 +104,6 @@
     ]
     for load in loads[:3] + first:
         load.start()
-
-    barrier = pltpu.get_barrier_semaphore()
-
-    def greet(d, _):
-        pl.semaphore_signal(
-            barrier, inc=1, device_id=(lax.rem(c + d, nc), z), device_id_type=MESH
-        )
-        return 0
-
-    lax.fori_loop(1, nc, greet, 0)
-    right, left = lax.rem(z + 1, nz), lax.rem(z + nz - 1, nz)
-    for other in (right, left):
-        pl.semaphore_signal(barrier, inc=1, device_id=(c, other), device_id_type=MESH)
 
     loads[0].wait()
     loads[1].wait()
@@ -125,11 +126,6 @@
         wown[way] = wpart[way].astype(F32)
     pl.semaphore_wait(barrier, nc + 1)
 
-    def partner(n):
-        dx, dy, dk = STEPS[n]
-        x, y = lax.rem(px + dx + SIDE, SIDE), lax.rem(py + dy + SIDE, SIDE)
-        return (y * SIDE + x) * 2 + lax.rem(core + dk, 2)
-
     def to_owner(g, t):
         return pltpu.make_async_remote_copy(
             sbuf.at[g, :, t], rbuf.at[g, :, c], asend.at[g], arecv.at[g],
@@ -195,7 +191,6 @@
             device_id=(c, right), device_id_type=MESH,
         )
 
-    others = [partner(n) for n in range(nc - 1)]
     for t in others:
         to_owner(0, t).start()
     for way in range(2):
@@ -235,28 +230,29 @@
 
         def combine(tile, _):
             for hi in range(nc // SUB):
-                acc_r = [None] * SUB
-                acc_i = [None] * SUB
+                acc = [[None] * SUB for _ in range(3)]
                 for lo in range(hi + 1):
-                    srcs = [(sb[tile, 0, lo * SUB + n], sb[tile, 1, lo * SUB + n]) for n in range(SUB)]
+                    srcs = []
+                    for n in range(SUB):
+                        sr, si = sb[tile, 0, lo * SUB + n], sb[tile, 1, lo * SUB + n]
+                        srcs.append((sr + si, sr, si))
                     base = (hi - lo) * SUB
                     for diff in range(1 - SUB, SUB):
                         if base + diff < 0:
                             continue
                         fr = gb[tile, 0, SUB + base + diff]
                         fi = gb[tile, 1, SUB + base + diff]
+                        terms = (fr, fi - fr, fr + fi)
                         for n in range(SUB):
                             a = n + diff
                             if a < 0 or a >= SUB:
                                 continue
-                            sr, si = srcs[n]
-                            pr = sr * fr - si * fi
-                            pi = sr * fi + si * fr
-                            acc_r[a] = pr if acc_r[a] is None else acc_r[a] + pr
-                            acc_i[a] = pi if acc_i[a] is None else acc_i[a] + pi
+                            for m in range(3):
+                                prod = srcs[n][m] * terms[m]
+                                acc[m][a] = prod if acc[m][a] is None else acc[m][a] + prod
                 for a in range(SUB):
-                    zb[0, tile, hi * SUB + a] = acc_r[a]
-                    zb[1, tile, hi * SUB + a] = acc_i[a]
+                    zb[0, tile, hi * SUB + a] = acc[0][a] - acc[2][a]
+                    zb[1, tile, hi * SUB + a] = acc[0][a] + acc[1][a]
             return 0
 
         lax.fori_loop(0, 2, combine, 0)

time: 73.4 us -> 72.4 us (0.986)
  Pallas kernels: 72.6 us -> 71.4 us
    pallas_call x1, Pallas kernels: 72.6 us -> 71.4 us  [body(): pl.pallas_call(functools.partial(kernel, nc, nz), out_shape=jax.ShapeDtyp...]
where the time goes in v5:
time: 72.4 us; the launch traced here: 72.2 us
  Pallas kernels  71.4 us (99%)
    pallas_call x1, Pallas kernels, body(): pl.pallas_call(functools.partial(kernel, nc, nz), out_shape=jax.ShapeDtyp...  71.4 us

profile of v5, /device:TPU:1, one launch (start us, length us, event | category | flops | bytes accessed | tf_op | source)
XLA Modules:
  0.0 72.2 jit_solution(11621345026214192580)
XLA Ops:
  0.0 71.4 %shard_map.100 = bf16[256,512]{1,0:T(8,128)(2,1)S(1)} custom-call(bf16[256,512]{1,0:T(8,128)(2,1)} %q_hbm.1, bf16[256,512]{1,0:T(8,128)(2,1)} %k_hbm.1, bf16[256,512]{1,0:T(8,128)(2,1)} %v_hbm.1, f32[256,512]{1,0:T(8,128)} %f_hbm.1, f32[1,512]{1,0:T(1,128)} %bitcast.1, bf16[256,512]{1,0:T(8,128)(2,1)} %constant.8.clone.th_hbm, ...), custom_call_target="tpu_custom_call" | custom-call | tf_op jit(solution)/shard_map/pallas_call | solution.py:368
  71.5 0.7 copy.12

commit v6 on v5

--- a/solution.py
+++ b/solution.py
@@ -255,7 +255,8 @@
                     zb[1, tile, hi * SUB + a] = acc[0][a] + acc[1][a]
             return 0
 
-        lax.fori_loop(0, 2, combine, 0)
+        combine(0, 0)
+        combine(1, 0)
         whole = jnp.concatenate(
             [zb[p, t].reshape(nc * SUB, LANES) for p in range(2) for t in range(2)], axis=1
         )

time: 72.4 us -> 72.2 us (level)
  no operation moved by 1% of the time
where the time goes in v6:
time: 72.2 us; the launch traced here: 72 us
  Pallas kernels  71.3 us (99%)
    pallas_call x1, Pallas kernels, body(): pl.pallas_call(functools.partial(kernel, nc, nz), out_shape=jax.ShapeDtyp...  71.3 us

profile of v6, /device:TPU:1, one launch (start us, length us, event | category | flops | bytes accessed | tf_op | source)
XLA Modules:
  0.0 72.0 jit_solution(3154601134360869565)
XLA Ops:
  0.0 71.3 %shard_map.100 = bf16[256,512]{1,0:T(8,128)(2,1)S(1)} custom-call(bf16[256,512]{1,0:T(8,128)(2,1)} %q_hbm.1, bf16[256,512]{1,0:T(8,128)(2,1)} %k_hbm.1, bf16[256,512]{1,0:T(8,128)(2,1)} %v_hbm.1, f32[256,512]{1,0:T(8,128)} %f_hbm.1, f32[1,512]{1,0:T(1,128)} %bitcast.1, bf16[256,512]{1,0:T(8,128)(2,1)} %constant.8.clone.th_hbm, ...), custom_call_target="tpu_custom_call" | custom-call | tf_op jit(solution)/shard_map/pallas_call | solution.py:369
  71.3 0.7 copy.12
